TPU v7x, 256 devices: a whole 4x4x8 slice. The times are simulated.
256 devices in a mesh: tm: 8 (over z), space: 32 (over x, y, core).
Axes of the slice: x: 4, y: 4, z: 8, core: 2. Of those that a mesh axis runs over, the one named last changes fastest.
Arguments:
- snapshots: float32 [4096, 32768], P('tm', 'space')
- weights: float32 [32768], P('space'), may hold values from 0.25 to 4
Outputs:
- modes: float32 [64, 2, 4, 32768], P('tm', None, None, 'space')
- cross_spectra: float32 [64, 2, 31, 31], P('tm')
All inputs are finite; a program needn't handle non-finite values.
Results may differ from a plain program's by a relative error of at most 0.00014.
Values sent between devices are 32-bit elements; how exact they have to be, the bound alone decides.
A program may use at most 128 MiB of HBM per device.

v0:
```python
import math

import jax
import jax.numpy as jnp
from jax import lax
from jax.sharding import PartitionSpec as P

NFFT = 256
STRIDE = 128
NFREQ = 64
NMODE = 4


HIGH = lax.Precision.HIGHEST


def dft_table(length, freqs):
    steps = jnp.arange(length, dtype=jnp.int32)
    orders = jnp.arange(freqs, dtype=jnp.int32)
    phase = (steps[:, None] * orders[None, :] % length).astype(jnp.float32)
    angle = 2.0 * math.pi * phase / length
    window = 0.5 - 0.5 * jnp.cos(2.0 * math.pi * steps.astype(jnp.float32) / length)
    norm = math.sqrt(3.0 * length / 8.0)
    real_part = window[:, None] * jnp.cos(angle) / norm
    imag_part = -window[:, None] * jnp.sin(angle) / norm
    return jnp.stack([real_part, imag_part], axis=2)


def rebuild(spectra, gram_real, gram_imag):
    nblocks = gram_real.shape[1]
    rows = jnp.arange(nblocks, dtype=jnp.float32)
    orders = jnp.arange(NMODE, dtype=jnp.float32)
    basis = jnp.cos(math.pi * (rows[:, None] + 0.5) * orders[None, :] / nblocks)
    trace = jnp.trace(gram_real, axis1=1, axis2=2) + 1e-06
    scale = (nblocks / trace)[:, None, None]
    first_real = scale * jnp.einsum("fab,bm->fam", gram_real, basis, precision=HIGH)
    first_imag = scale * jnp.einsum("fab,bm->fam", gram_imag, basis, precision=HIGH)
    second_real = scale * (
        jnp.einsum("fab,fbm->fam", gram_real, first_real, precision=HIGH)
        - jnp.einsum("fab,fbm->fam", gram_imag, first_imag, precision=HIGH)
    )
    second_imag = scale * (
        jnp.einsum("fab,fbm->fam", gram_real, first_imag, precision=HIGH)
        + jnp.einsum("fab,fbm->fam", gram_imag, first_real, precision=HIGH)
    )
    spec_real = spectra[:, 0]
    spec_imag = spectra[:, 1]
    mode_real = (
        jnp.einsum("fbx,fbm->fmx", spec_real, second_real, precision=HIGH)
        - jnp.einsum("fbx,fbm->fmx", spec_imag, second_imag, precision=HIGH)
    ) / nblocks
    mode_imag = (
        jnp.einsum("fbx,fbm->fmx", spec_real, second_imag, precision=HIGH)
        + jnp.einsum("fbx,fbm->fmx", spec_imag, second_real, precision=HIGH)
    ) / nblocks
    return jnp.stack([mode_real, mode_imag], axis=1)


def local(snapshots, weights):
    local_steps, points = snapshots.shape
    tm_count = lax.axis_size("tm")
    space_count = lax.axis_size("space")
    strides = local_steps // STRIDE
    table = dft_table(NFFT, NFREQ)
    halves = jnp.stack([table[:STRIDE], table[STRIDE:]], axis=1).reshape(STRIDE, 4 * NFREQ)
    pieces = snapshots.reshape(strides, STRIDE, points)
    partial_value = jnp.einsum("nc,snx->csx", halves, pieces, precision=HIGH).reshape(
        2, NFREQ, 2, strides, points
    )
    opening = partial_value[0]
    closing = partial_value[1]
    empty_tail = jnp.zeros((NFREQ, 2, 1, points), jnp.float32)
    owned = opening + jnp.concatenate([closing[:, :, 1:, :], empty_tail], axis=2)
    placed = jnp.concatenate([closing[:, :, :1, :], owned], axis=2)
    canvas = jnp.zeros((NFREQ, 2, strides * tm_count + 1, points), jnp.float32)
    offset = lax.axis_index("tm") * strides
    zero_index = jnp.zeros((), jnp.int32)
    canvas = lax.dynamic_update_slice(canvas, placed, (zero_index, zero_index, offset, zero_index))
    spectra = lax.psum_scatter(canvas[:, :, 1:, :], "tm", scatter_dimension=0, tiled=True)
    freqs_own = spectra.shape[0]
    nblocks = spectra.shape[2] - 1
    kept = spectra[:, :, :nblocks, :]
    stacked = kept.reshape(freqs_own, 2 * nblocks, points)
    products = jnp.einsum(
        "fax,fbx->fab", stacked, stacked * weights[None, None, :], precision=HIGH
    ) / (points * space_count)
    gram_real = products[:, :nblocks, :nblocks] + products[:, nblocks:, nblocks:]
    gram_imag = products[:, :nblocks, nblocks:] - products[:, nblocks:, :nblocks]
    local_gram = jnp.stack([gram_real, gram_imag], axis=1)

    def summed_one(carry, single):
        return (carry, lax.psum(single, "space"))

    unused, cross_spectra = lax.scan(summed_one, jnp.zeros((), jnp.float32), local_gram)
    modes = rebuild(kept, cross_spectra[:, 0], cross_spectra[:, 1])
    return (modes, cross_spectra)


def solution(mesh):
    return jax.shard_map(
        local,
        mesh=mesh,
        in_specs=(P("tm", "space"), P("space")),
        out_specs=(P("tm", None, None, "space"), P("tm", None, None, None)),
        check_vma=False,
    )
```

profile of v0, /device:TPU:1, one launch (start us, length us, event | category | flops | bytes accessed | tf_op | source)
XLA Modules:
  0.0 1271.1 jit_solution(8353560039651112233)
XLA Ops:
  7.8 1.0 copy-done
  8.8 3.5 fusion.39
  12.2 2.3 fusion.38
  14.5 2.5 squeeze.22
  17.0 0.7 slice.73
  17.7 0.8 copy-done.2
  18.5 1.1 copy.57
  19.6 3.5 squeeze.23
  23.7 3.2 copy_add_fusion
  26.9 2.8 pad_maximum_fusion
  29.7 9.7 broadcast_in_dim.30
  39.4 21.6 %dynamic_update_slice.7 = f32[64,2,33,1024]{3,2,0,1:T(8,128)} dynamic-update-slice(f32[64,2,33,1024]{3,2,0,1:T(8,128)} %broadcast_in_dim.30, f32[64,2,5,1024]{3,2,0,1:T(8,128)} %pad_maximum_fusion, s32[]{:T(128)} %copy.80, s32[]{:T(128)} %copy.80, s32[]{:T(128)S(6)} %select_n.29, s32[]{:T(128)} %copy.80) | dynamic-update-slice | bytes 5242884 | tf_op jit(solution)/shard_map/dynamic_update_slice | solution.py:78
  61.0 8.0 slice.74
  69.0 1.8 copy.53
  70.8 11.7 copy.60
  82.6 177.6 %reduce-scatter.5.cloned.1.call-done = f32[8,65536]{1,0:T(8,128)} async-done(((f32[64,65536]{1,0:T(8,128)}), f32[8,65536]{1,0:T(8,128)}) %reduce-scatter.5.cloned.1.call-update) | async-done | bytes 2097168
  260.2 1.8 slice.75
  262.2 4.3 fusion.3
  266.9 990.0 %while.10 = (s32[]{:T(128)}, f32[8,2,31,31]{3,1,2,0:T(2,128)S(1)}, f32[8,2,31,31]{3,1,2,0:T(2,128)S(1)}, s32[]{:T(128)}) while((s32[]{:T(128)}, f32[8,2,31,31]{3,1,2,0:T(2,128)S(1)}, f32[8,2,31,31]{3,1,2,0:T(2,128)S(1)}, s32[]{:T(128)}) %tuple.36), condition=%wide.region_3.4_spmd, body=%wide.region_1.3_spmd.sunk | while | flops 1924 | bytes 94301 | solution.py:94
  266.9 123.2 %psum.8 = f32[1,2,31,31]{3,1,2,0:T(2,128)S(1)} all-reduce(f32[1,2,31,31]{3,1,2,0:T(2,128)S(1)} %constant_dynamic-slice_fusion.2), channel_id=1, replica_groups=mesh['tm'=8,'space'=32] {'space'}, use_global_device_ids=true, to_apply=%region_2.2 | all-reduce | flops 1922 | bytes 15376 | tf_op jit(solution)/shard_map/while/body/eval_jaxpr/psum | solution.py:92
  390.2 123.8 %psum.8 = f32[1,2,31,31]{3,1,2,0:T(2,128)S(1)} all-reduce(f32[1,2,31,31]{3,1,2,0:T(2,128)S(1)} %constant_dynamic-slice_fusion.2), channel_id=1, replica_groups=mesh['tm'=8,'space'=32] {'space'}, use_global_device_ids=true, to_apply=%region_2.2 | all-reduce | flops 1922 | bytes 15376 | tf_op jit(solution)/shard_map/while/body/eval_jaxpr/psum | solution.py:92
  514.0 123.8 %psum.8 = f32[1,2,31,31]{3,1,2,0:T(2,128)S(1)} all-reduce(f32[1,2,31,31]{3,1,2,0:T(2,128)S(1)} %constant_dynamic-slice_fusion.2), channel_id=1, replica_groups=mesh['tm'=8,'space'=32] {'space'}, use_global_device_ids=true, to_apply=%region_2.2 | all-reduce | flops 1922 | bytes 15376 | tf_op jit(solution)/shard_map/while/body/eval_jaxpr/psum | solution.py:92
  637.8 123.8 %psum.8 = f32[1,2,31,31]{3,1,2,0:T(2,128)S(1)} all-reduce(f32[1,2,31,31]{3,1,2,0:T(2,128)S(1)} %constant_dynamic-slice_fusion.2), channel_id=1, replica_groups=mesh['tm'=8,'space'=32] {'space'}, use_global_device_ids=true, to_apply=%region_2.2 | all-reduce | flops 1922 | bytes 15376 | tf_op jit(solution)/shard_map/while/body/eval_jaxpr/psum | solution.py:92
  761.6 123.8 %psum.8 = f32[1,2,31,31]{3,1,2,0:T(2,128)S(1)} all-reduce(f32[1,2,31,31]{3,1,2,0:T(2,128)S(1)} %constant_dynamic-slice_fusion.2), channel_id=1, replica_groups=mesh['tm'=8,'space'=32] {'space'}, use_global_device_ids=true, to_apply=%region_2.2 | all-reduce | flops 1922 | bytes 15376 | tf_op jit(solution)/shard_map/while/body/eval_jaxpr/psum | solution.py:92
  885.5 123.8 %psum.8 = f32[1,2,31,31]{3,1,2,0:T(2,128)S(1)} all-reduce(f32[1,2,31,31]{3,1,2,0:T(2,128)S(1)} %constant_dynamic-slice_fusion.2), channel_id=1, replica_groups=mesh['tm'=8,'space'=32] {'space'}, use_global_device_ids=true, to_apply=%region_2.2 | all-reduce | flops 1922 | bytes 15376 | tf_op jit(solution)/shard_map/while/body/eval_jaxpr/psum | solution.py:92
  1009.3 123.8 %psum.8 = f32[1,2,31,31]{3,1,2,0:T(2,128)S(1)} all-reduce(f32[1,2,31,31]{3,1,2,0:T(2,128)S(1)} %constant_dynamic-slice_fusion.2), channel_id=1, replica_groups=mesh['tm'=8,'space'=32] {'space'}, use_global_device_ids=true, to_apply=%region_2.2 | all-reduce | flops 1922 | bytes 15376 | tf_op jit(solution)/shard_map/while/body/eval_jaxpr/psum | solution.py:92
  1133.1 123.8 %psum.8 = f32[1,2,31,31]{3,1,2,0:T(2,128)S(1)} all-reduce(f32[1,2,31,31]{3,1,2,0:T(2,128)S(1)} %constant_dynamic-slice_fusion.2), channel_id=1, replica_groups=mesh['tm'=8,'space'=32] {'space'}, use_global_device_ids=true, to_apply=%region_2.2 | all-reduce | flops 1922 | bytes 15376 | tf_op jit(solution)/shard_map/while/body/eval_jaxpr/psum | solution.py:92
  1257.1 0.6 convolution_multiply_fusion.1
  1257.7 0.6 convolution_multiply_fusion
  1259.4 1.2 copy.61
  1260.9 0.6 fusion.15
  1263.5 0.7 copy.52
  (55 shorter events, 5.2 us)
Async XLA Ops:
  7.2 1.6 copy-start
  7.2 253.0 %reduce-scatter.5.cloned.1.call-start = ((), (), s32[]{:S(2)}) async-start(), calls=%async_computation.1 | async-start | bytes 18874368
  17.0 1.5 copy-start.2
  19.6 3.5 slice-start
  82.6 179.4 %copy-start.5 = (f32[1024]{0:T(1024)S(1)}, f32[1024]{0:T(1024)}, u32[]{:S(2)}) copy-start(f32[1024]{0:T(1024)} %param.5) | copy-start | bytes 12292
  266.5 992.8 %copy-start.3 = (f32[8,65536]{1,0:T(8,128)S(1)}, f32[8,65536]{1,0:T(8,128)}, u32[]{:S(2)}) copy-start(f32[8,65536]{1,0:T(8,128)} %reduce-scatter.5.cloned.1.call-done) | copy-start | bytes 6291460
  1256.9 3.7 copy-start.4
  1261.6 2.7 copy-start.1
Sparse Core Ops, SparseCore 0:
  82.7 177.4 reduce-scatter.4
where the time goes:
time: 1270 us
  blocking collectives  990 us (78%)
  waiting for transfers between devices  178 us (14%)
  local copies, waits for them, and re-layouts  69.4 us (5%)
  between operations  14.3 us (1%)
  matrix products  12.8 us (1%)
    psum x8, blocking collectives, summed_one(): return (carry, lax.psum(single, 'space'))  990 us
    unnamed x2, waiting for transfers between devices  178 us
  transfers between devices with their start and end apart: 1, of which 1 were waited for; matrix products, arithmetic and copies ran while one was open for 0% of the time, Pallas kernels for 0%

commit v1 on v0

v1 whole, which is shorter than its diff:
```python
import functools
import math

import jax
import jax.numpy as jnp
import ml_dtypes
import numpy as np
from jax import lax
from jax.experimental import pallas as pl
from jax.experimental.pallas import tpu as pltpu
from jax.sharding import PartitionSpec as P

NFFT = 256
STRIDE = 128
NFREQ = 64
NMODE = 4
NB = 31
TM = 8
OWN = NFREQ // TM
CHIPS = 16
LAG = 2
MESH = pl.DeviceIdType.MESH
F32 = jnp.float32
BF16 = jnp.bfloat16
HIGHEST = lax.Precision.HIGHEST
NN = (((1,), (0,)), ((), ()))
NT = (((1,), (1,)), ((), ()))


def row_plan():
    rows = []
    for d in range(TM):
        if d <= 3:
            rows.append((d, "close"))
        elif d == 4:
            rows.append((0, "open"))
        else:
            rows.append((d, "open"))
        rows.extend((d, j) for j in range(3))
    rows.extend((d, "open") for d in (1, 2, 3, 4))
    rows.extend((d, "close") for d in (7, 6, 5, 4))
    return rows


def tables(strides):
    steps = np.arange(NFFT)
    window = 0.5 - 0.5 * np.cos(2.0 * np.pi * steps / NFFT)
    angle = 2.0 * np.pi * ((steps[None, :] * np.arange(NFREQ)[:, None]) % NFFT) / NFFT
    norm = math.sqrt(3.0 * NFFT / 8.0)
    wave = np.stack([window * np.cos(angle) / norm, -window * np.sin(angle) / norm], axis=1)
    plan = row_plan()
    full = np.zeros((TM, OWN, 2 * len(plan), strides * STRIDE), np.float32)
    for me in range(TM):
        for place, (d, kind) in enumerate(plan):
            owner = (me + d) % TM
            part = wave[owner * OWN : (owner + 1) * OWN]
            row = full[me, :, 2 * place : 2 * place + 2]
            if kind == "close":
                row[:, :, :STRIDE] = part[:, :, STRIDE:]
            elif kind == "open":
                row[:, :, (strides - 1) * STRIDE :] = part[:, :, :STRIDE]
            else:
                row[:, :, kind * STRIDE : kind * STRIDE + NFFT] = part
    high = full.astype(ml_dtypes.bfloat16)
    low = (full - high.astype(np.float32)).astype(ml_dtypes.bfloat16)
    return np.concatenate([high, low], axis=2)


def block_order(me):
    order = []
    for slot in range(TM):
        source = me + slot
        if slot == 4:
            order.append(4 * me + 3)
        elif slot in (1, 2, 3):
            order.append(4 * source + 3)
        else:
            order.append(4 * source - 1)
        order.extend(4 * source + j for j in range(3))
    return [b % (NB + 1) for b in order]


PACK_V0, PACK_COL, PACK_ROW, PACK_C0, PACK_C1, PACK_END = 0, 8, 136, 168, 232, 296


def small_tables():
    pack = np.zeros((TM, PACK_END, 128), np.float32)
    b = np.arange(NB)
    m = np.arange(NMODE)
    basis = np.cos(np.pi * (b[:, None] + 0.5) * m[None, :] / NB)
    swap = np.zeros((64, 64), np.float32)
    for i in range(32):
        swap[2 * i + 1, 2 * i] = 1.0
        swap[2 * i, 2 * i + 1] = -1.0
    eye = np.eye(64, dtype=np.float32)
    for me in range(TM):
        for place, block in enumerate(block_order(me)):
            if block < NB:
                pack[me, PACK_V0 : PACK_V0 + 4, 2 * place] = basis[block]
                pack[me, PACK_V0 + 4 : PACK_V0 + 8, 2 * place + 1] = basis[block]
            pack[me, PACK_COL + 2 * place, block] = 1.0
            pack[me, PACK_COL + 2 * place + 1, 32 + block] = 1.0
            pack[me, PACK_ROW + block, place] = 1.0
        pack[me, PACK_C0 : PACK_C0 + 64, :64] = eye
        pack[me, PACK_C0 : PACK_C0 + 64, 64:] = -swap
        pack[me, PACK_C1 : PACK_C1 + 64, :64] = swap
        pack[me, PACK_C1 : PACK_C1 + 64, 64:] = eye
    return pack


def split(value):
    high = value.astype(BF16)
    return high, (value - high.astype(F32)).astype(BF16)


def dot(a, b, dims=NN, precision=None):
    return lax.dot_general(a, b, dims, precision=precision, preferred_element_type=F32)


def kernel(
    x_hbm, w_ref, table_hbm, pack_hbm, modes_ref, cross_ref,
    x, xh, xl, table, pack, made, halo_out, halo_in, got, ah, al, gram, core_out, core_in, chip_all,
    load_sem, table_sem, halo_ssem, halo_rsem, send_sem, recv_sem, core_ssem, core_rsem, chip_ssem, chip_rsem,
):
    points = x.shape[1]
    me = lax.axis_index("tm")
    space = lax.axis_index("space")
    core = lax.rem(space, 2)
    chip = space // 2
    cx = chip // 4
    cy = lax.rem(chip, 4)

    def along(d):
        return (lax.rem(me + d + TM, TM), space)

    others = [(i, j) for i in range(4) for j in range(4) if i or j]
    others.sort(key=lambda ij: -(min(ij[0], 4 - ij[0]) + min(ij[1], 4 - ij[1])))

    def chip_of(i, j):
        return lax.rem(cx + i, 4) * 4 + lax.rem(cy + j, 4)

    def across(i, j):
        return (me, chip_of(i, j) * 2 + core)

    mate = (me, chip * 2 + 1 - core)

    barrier = pltpu.get_barrier_semaphore()
    for d in range(1, TM):
        pl.semaphore_signal(barrier, inc=1, device_id=along(d), device_id_type=MESH)
    for i, j in others:
        pl.semaphore_signal(barrier, inc=1, device_id=across(i, j), device_id_type=MESH)
    pl.semaphore_signal(barrier, inc=1, device_id=mate, device_id_type=MESH)

    pieces = x.shape[0] // STRIDE

    def load_x(p):
        rows = pl.ds(p * STRIDE, STRIDE)
        return pltpu.make_async_copy(x_hbm.at[rows], x.at[rows], load_sem.at[p])

    def load_pack():
        return pltpu.make_async_copy(pack_hbm.at[me], pack, load_sem.at[pieces])

    def load_table(c):
        return pltpu.make_async_copy(table_hbm.at[me, c], table.at[c], table_sem.at[c])

    for p in range(pieces):
        load_x(p).start()
    load_table(0).start()
    load_pack().start()
    for c in range(1, OWN):
        load_table(c).start()
    for p in range(pieces):
        load_x(p).wait()
        rows = pl.ds(p * STRIDE, STRIDE)
        high, low = split(x[rows, :])
        xh[rows, :] = high
        xl[rows, :] = low
    load_pack().wait()

    def halo_copy(c, side):
        return pltpu.make_async_remote_copy(
            src_ref=halo_out.at[c, side], dst_ref=halo_in.at[c, side],
            send_sem=halo_ssem.at[c, side], recv_sem=halo_rsem.at[c, side],
            device_id=along(1 if side == 0 else -1), device_id_type=MESH,
        )

    def tile_copy(c, d):
        slot = (TM - d) % TM
        rows = pl.ds(2, 6) if d == 4 else pl.ds(0, 8)
        return pltpu.make_async_remote_copy(
            src_ref=made.at[c, d, rows], dst_ref=got.at[c, slot, rows],
            send_sem=send_sem.at[c, d], recv_sem=recv_sem.at[c, slot],
            device_id=along(d), device_id_type=MESH,
        )

    def core_copy(c):
        return pltpu.make_async_remote_copy(
            src_ref=core_out.at[c], dst_ref=core_in.at[c],
            send_sem=core_ssem.at[c], recv_sem=core_rsem.at[c],
            device_id=mate, device_id_type=MESH,
        )

    def chip_copy(c, n, i, j):
        return pltpu.make_async_remote_copy(
            src_ref=chip_all.at[c, chip], dst_ref=chip_all.at[c, chip],
            send_sem=chip_ssem.at[c, n], recv_sem=chip_rsem.at[c, chip],
            device_id=across(i, j), device_id_type=MESH,
        )

    def chip_arrival(c, n, i, j):
        source = chip_of(i, j)
        return pltpu.make_async_remote_copy(
            src_ref=chip_all.at[c, source], dst_ref=chip_all.at[c, source],
            send_sem=chip_ssem.at[c, n], recv_sem=chip_rsem.at[c, source],
            device_id=across(i, j), device_id_type=MESH,
        )

    def make(c):
        load_table(c).wait()
        for n in range(points // 256):
            columns = pl.ds(n * 256, 256)
            both = dot(table[c], xh[:, columns])
            value = both[:80] + both[80:] + dot(table[c, :80, :], xl[:, columns])
            for d in range(TM):
                made[c, d, :, columns] = value[8 * d : 8 * d + 8]
            halo_out[c, 0, :, columns] = value[64:72]
            halo_out[c, 1, :, columns] = value[72:80]

    def send_first(c):
        halo_copy(c, 0).start()
        halo_copy(c, 1).start()
        tile_copy(c, 4).start()

    def send_rest(c):
        halo_copy(c, 0).wait_recv()
        halo_copy(c, 1).wait_recv()
        first = me == 0
        last = me == TM - 1
        for d in range(4):
            total = made[c, d, 0:2, :] + halo_in[c, 0, 2 * d : 2 * d + 2, :]
            made[c, d, 0:2, :] = jnp.where(first, 0.0, total)
        for n, d in enumerate((4, 7, 6, 5)):
            total = made[c, d, 0:2, :] + halo_in[c, 1, 2 * n : 2 * n + 2, :]
            made[c, d, 0:2, :] = jnp.where(last, 0.0, total)
        for d in (5, 3, 6, 2, 7, 1):
            tile_copy(c, d).start()

    def correlate(c):
        for d in (4, 5, 3, 6, 2, 7, 1):
            tile_copy(c, d).wait_recv()
        own_rows = lax.broadcasted_iota(jnp.int32, (8, points), 0) < 2
        tiles = [made[c, 0]]
        for slot in range(1, TM):
            tile = got[c, slot]
            if slot == 4:
                tile = jnp.where(own_rows, made[c, 4], tile)
            tiles.append(tile)
        value = jnp.concatenate(tiles, axis=0)
        high, low = split(value)
        ah[c] = high
        al[c] = low
        whigh, wlow = split(value * w_ref[...])
        gram[...] = (
            dot(high, whigh, NT) + dot(high, wlow, NT) + dot(low, whigh, NT)
        )
        even = gram[pl.ds(0, 32, stride=2), :]
        odd = gram[pl.ds(1, 32, stride=2), :]
        core_out[c] = (
            dot(even, pack[PACK_C0 : PACK_C0 + 64, :], precision=HIGHEST)
            + dot(odd, pack[PACK_C1 : PACK_C1 + 64, :], precision=HIGHEST)
        )
        core_copy(c).start()

    def spread(c):
        core_copy(c).wait_recv()
        chip_all[c, chip] = core_out[c] + core_in[c]
        for n, (i, j) in enumerate(others):
            chip_copy(c, n, i, j).start()

    def finish(c):
        for n, (i, j) in enumerate(others):
            chip_arrival(c, n, i, j).wait_recv()
        parts = [chip_all[c, n] for n in range(CHIPS)]
        while len(parts) > 1:
            parts = [parts[n] + parts[n + 1] for n in range(0, len(parts), 2)]
        total = parts[0] / (points * 2 * CHIPS)
        rows = lax.broadcasted_iota(jnp.int32, total.shape, 0)
        lanes = lax.broadcasted_iota(jnp.int32, total.shape, 1)
        trace = jnp.sum(jnp.where(lanes == 2 * rows, total, 0.0)) + 1e-06
        scale = NB / trace
        wide = jnp.concatenate([total, pltpu.roll(total, 64, 1)], axis=0)[:, :64]
        one = scale * dot(pack[PACK_V0 : PACK_V0 + 8, :64], wide, NT, HIGHEST)
        two = scale * dot(one, wide, NN, HIGHEST)
        high, low = split(two)
        built = dot(high, ah[c]) + dot(high, al[c]) + dot(low, ah[c])
        modes_ref[c] = built / NB
        ordered = dot(total, pack[PACK_COL : PACK_COL + 128, :], precision=HIGHEST)
        ordered = dot(pack[PACK_ROW : PACK_ROW + 32, :32], ordered, precision=HIGHEST)
        cross_ref[c, 0] = ordered[:NB, :NB]
        cross_ref[c, 1] = pltpu.roll(ordered, 96, 1)[:NB, :NB]

    make(0)
    pl.semaphore_wait(barrier, (TM - 1) + len(others) + 1)
    send_first(0)

    def step(s, carry):
        @pl.when(s < OWN)
        def _():
            make(s)
            send_first(s)

        @pl.when(s <= OWN)
        def _():
            send_rest(s - 1)

        @pl.when((s >= LAG) & (s < OWN + LAG))
        def _():
            correlate(s - LAG)
            spread(s - LAG)

        @pl.when(s >= LAG + 1)
        def _():
            finish(s - LAG - 1)

        return carry

    lax.fori_loop(1, OWN + LAG + 1, step, 0)

    def drain(c, carry):
        halo_copy(c, 0).wait_send()
        halo_copy(c, 1).wait_send()
        for d in range(1, TM):
            tile_copy(c, d).wait_send()
        core_copy(c).wait_send()
        for n, (i, j) in enumerate(others):
            chip_copy(c, n, i, j).wait_send()
        return carry

    lax.fori_loop(0, OWN, drain, 0)


def local(snapshots, weights):
    steps, points = snapshots.shape
    table = jnp.asarray(tables(steps // STRIDE))
    pack = jnp.asarray(small_tables())
    rows = table.shape[2]
    any_space = pl.BlockSpec(memory_space=pl.ANY)
    vmem = pl.BlockSpec(memory_space=pltpu.VMEM)
    dma = pltpu.SemaphoreType.DMA
    modes, cross = pl.pallas_call(
        kernel,
        out_shape=(
            jax.ShapeDtypeStruct((OWN, 2 * NMODE, points), F32),
            jax.ShapeDtypeStruct((OWN, 2, NB, NB), F32),
        ),
        in_specs=[any_space, vmem, any_space, any_space],
        out_specs=(vmem, vmem),
        scratch_shapes=[
            pltpu.VMEM((steps, points), F32),
            pltpu.VMEM((steps, points), BF16),
            pltpu.VMEM((steps, points), BF16),
            pltpu.VMEM((OWN, rows, steps), BF16),
            pltpu.VMEM((PACK_END, 128), F32),
            pltpu.VMEM((OWN, TM, 8, points), F32),
            pltpu.VMEM((OWN, 2, 8, points), F32),
            pltpu.VMEM((OWN, 2, 8, points), F32),
            pltpu.VMEM((OWN, TM, 8, points), F32),
            pltpu.VMEM((OWN, 64, points), BF16),
            pltpu.VMEM((OWN, 64, points), BF16),
            pltpu.VMEM((64, 64), F32),
            pltpu.VMEM((OWN, 32, 128), F32),
            pltpu.VMEM((OWN, 32, 128), F32),
            pltpu.VMEM((OWN, CHIPS, 32, 128), F32),
            dma((steps // STRIDE + 1,)),
            dma((OWN,)),
            dma((OWN, 2)),
            dma((OWN, 2)),
            dma((OWN, TM)),
            dma((OWN, TM)),
            dma((OWN,)),
            dma((OWN,)),
            dma((OWN, CHIPS)),
            dma((OWN, CHIPS)),
        ],
        compiler_params=pltpu.CompilerParams(
            collective_id=0, has_side_effects=True, vmem_limit_bytes=48 << 20
        ),
        cost_estimate=pl.CostEstimate(flops=4 << 30, bytes_accessed=8 << 20, transcendentals=0),
        name="spod",
    )(snapshots, weights.reshape(1, points), table, pack)
    return modes.reshape(OWN, 2, NMODE, points), cross


def solution(mesh):
    return jax.shard_map(
        local,
        mesh=mesh,
        in_specs=(P("tm", "space"), P("space")),
        out_specs=(P("tm", None, None, "space"), P("tm", None, None, None)),
        check_vma=False,
    )
```

time: 1270 us -> 79 us (0.06)
  blocking collectives: 990 us -> 0 us
  waiting for transfers between devices: 178 us -> 0 us
  Pallas kernels: 0 us -> 73 us
  local copies, waits for them, and re-layouts: 69.4 us -> 5.22 us
  between operations: 14.3 us -> 0.65 us
  matrix products: 12.8 us -> 0 us
    psum x8 -> x0, blocking collectives: 990 us -> none  [summed_one(): return (carry, lax.psum(single, 'space'))]
    unnamed x2 -> x0, waiting for transfers between devices: 178 us -> none
    pallas_call x0 -> x1, Pallas kernels: none -> 73 us  [local(): pl.pallas_call(kernel, out_shape=(jax.ShapeDtypeStruct((OWN, 2 * NMODE, p...]
    dynamic_update_slice x9 -> x0, local copies, waits for them, and re-layouts: 21.7 us -> none  [the longest x1 21.6 us: local(): lax.dynamic_update_slice(canvas, placed, (zero_index, zero_index, offset,...]
    unnamed x18 -> x7, local copies, waits for them, and re-layouts: 18.9 us -> 4.45 us
    slice x6 -> x0, local copies, waits for them, and re-layouts: 12.8 us -> none  [the longest x1 8.03 us: local(): canvas[:, :, 1:, :]]
    dot_general x12 -> x0, matrix products: 12.8 us -> none  [the longest x1 4.28 us: local(): jnp.einsum('fax,fbx->fab', stacked, stacked * weights[None, None, :], pre...]
  transfers between devices with their start and end apart: 1 -> 0, of which waited for: 1 -> 0; matrix products, arithmetic and copies ran while one was open for 0% -> 0% of each run, Pallas kernels for 0% -> 0%
where the time goes in v1:
time: 79 us; the launch traced here: 78.8 us
  Pallas kernels  73 us (92%)
  local copies, waits for them, and re-layouts  5.22 us (7%)
    pallas_call x1, Pallas kernels, local(): pl.pallas_call(kernel, out_shape=(jax.ShapeDtypeStruct((OWN, 2 * NMODE, p...  73 us
    unnamed x7, local copies, waits for them, and re-layouts  4.45 us

profile of v1, /device:TPU:1, one launch (start us, length us, event | category | flops | bytes accessed | tf_op | source)
XLA Modules:
  0.0 78.8 jit_solution(9265267204275508669)
XLA Ops:
  0.6 0.0 copy-start
  0.6 1.6 %copy-done = f32[512,1024]{1,0:T(8,128)S(1)} copy-done((f32[512,1024]{1,0:T(8,128)S(1)}, f32[512,1024]{1,0:T(8,128)}, u32[]{:S(2)}) %copy-start) | copy-done | bytes 2097176
  2.2 0.0 copy-start.1
  2.2 0.7 copy-done.1
  2.9 0.0 copy-start.2
  2.9 1.3 %copy-done.2 = f32[8,296,128]{2,1,0:T(8,128)S(1)} copy-done((f32[8,296,128]{2,1,0:T(8,128)S(1)}, f32[8,296,128]{2,1,0:T(8,128)}, u32[]{:S(2)}) %copy-start.2) | copy-done | bytes 1212440
  4.2 73.0 %spod.1 = (f32[8,8,1024]{2,1,0:T(8,128)S(1)}, f32[8,2,31,31]{3,2,1,0:T(8,128)S(1)}) custom-call(f32[512,1024]{1,0:T(8,128)S(1)} %copy-done, f32[1,1024]{1,0:T(1,128)S(1)} %bitcast.1, bf16[8,8,160,512]{3,2,1,0:T(8,128)(2,1)} %constant.4.clone.table_hbm, f32[8,296,128]{2,1,0:T(8,128)S(1)} %copy-done.2), custom_call_target="tpu_custom_call" | custom-call | flops 4294967296 | bytes 8388608 | tf_op jit(solution)/shard_map/spod/pallas_call | solution.py:350
  77.2 0.8 reshape.11
  77.9 0.9 %copy.6 = f32[8,2,31,31]{3,1,2,0:T(2,128)} copy(f32[8,2,31,31]{3,2,1,0:T(8,128)S(1)} %get-tuple-element.7) | data formatting | bytes 123008
Async XLA Ops:
  0.6 1.6 %copy-start = (f32[512,1024]{1,0:T(8,128)S(1)}, f32[512,1024]{1,0:T(8,128)}, u32[]{:S(2)}) copy-start(f32[512,1024]{1,0:T(8,128)} %x_hbm.1) | copy-start | bytes 6291460
  2.2 0.7 copy-start.1
  2.9 1.3 %copy-start.2 = (f32[8,296,128]{2,1,0:T(8,128)S(1)}, f32[8,296,128]{2,1,0:T(8,128)}, u32[]{:S(2)}) copy-start(f32[8,296,128]{2,1,0:T(8,128)} %constant.5.clone.pack_hbm) | copy-start | bytes 3637252

commit v2 on v1

--- a/solution.py
+++ b/solution.py
@@ -19,6 +19,7 @@
 OWN = NFREQ // TM
 CHIPS = 16
 LAG = 2
+WAIT = 2
 MESH = pl.DeviceIdType.MESH
 F32 = jnp.float32
 BF16 = jnp.bfloat16
@@ -80,7 +81,7 @@
     return [b % (NB + 1) for b in order]
 
 
-PACK_V0, PACK_COL, PACK_ROW, PACK_C0, PACK_C1, PACK_END = 0, 8, 136, 168, 232, 296
+PACK_V0, PACK_COL, PACK_ROW, PACK_SWAP, PACK_END = 0, 8, 72, 104, 168
 
 
 def small_tables():
@@ -92,7 +93,6 @@
     for i in range(32):
         swap[2 * i + 1, 2 * i] = 1.0
         swap[2 * i, 2 * i + 1] = -1.0
-    eye = np.eye(64, dtype=np.float32)
     for me in range(TM):
         for place, block in enumerate(block_order(me)):
             if block < NB:
@@ -101,10 +101,7 @@
             pack[me, PACK_COL + 2 * place, block] = 1.0
             pack[me, PACK_COL + 2 * place + 1, 32 + block] = 1.0
             pack[me, PACK_ROW + block, place] = 1.0
-        pack[me, PACK_C0 : PACK_C0 + 64, :64] = eye
-        pack[me, PACK_C0 : PACK_C0 + 64, 64:] = -swap
-        pack[me, PACK_C1 : PACK_C1 + 64, :64] = swap
-        pack[me, PACK_C1 : PACK_C1 + 64, 64:] = eye
+        pack[me, PACK_SWAP : PACK_SWAP + 64, :64] = swap
     return pack
 
 
@@ -118,9 +115,9 @@
 
 
 def kernel(
-    x_hbm, w_ref, table_hbm, pack_hbm, modes_ref, cross_ref,
-    x, xh, xl, table, pack, made, halo_out, halo_in, got, ah, al, gram, core_out, core_in, chip_all,
-    load_sem, table_sem, halo_ssem, halo_rsem, send_sem, recv_sem, core_ssem, core_rsem, chip_ssem, chip_rsem,
+    x_hbm, w_hbm, table_hbm, pack_hbm, modes_ref, cross_ref,
+    x, w_ref, xh, xl, table, pack, made, halo_out, halo_in, got, ah, al, gram, core_out, core_in, chip_all,
+    load_sem, table_sem, send_sem, halo_rsem, tile_rsem, far_rsem, core_rsem, chip_rsem,
 ):
     points = x.shape[1]
     me = lax.axis_index("tm")
@@ -144,6 +141,31 @@
 
     mate = (me, chip * 2 + 1 - core)
 
+    pieces = points // 256
+
+    def load_x(p):
+        columns = pl.ds(p * 256, 256)
+        return pltpu.make_async_copy(x_hbm.at[:, columns], x.at[:, columns], load_sem.at[p])
+
+    def load_pack():
+        return pltpu.make_async_copy(pack_hbm.at[me], pack, load_sem.at[pieces])
+
+    def load_w():
+        return pltpu.make_async_copy(w_hbm, w_ref, load_sem.at[pieces + 1])
+
+    def load_table():
+        return pltpu.make_async_copy(table_hbm.at[me, 0], table.at[0], table_sem.at[0])
+
+    def load_tables():
+        rest = pl.ds(1, OWN - 1)
+        return pltpu.make_async_copy(table_hbm.at[me, rest], table.at[rest], table_sem.at[1])
+
+    load_table().start()
+    for p in range(pieces):
+        load_x(p).start()
+    load_pack().start()
+    load_w().start()
+    load_tables().start()
     barrier = pltpu.get_barrier_semaphore()
     for d in range(1, TM):
         pl.semaphore_signal(barrier, inc=1, device_id=along(d), device_id_type=MESH)
@@ -151,74 +173,60 @@
         pl.semaphore_signal(barrier, inc=1, device_id=across(i, j), device_id_type=MESH)
     pl.semaphore_signal(barrier, inc=1, device_id=mate, device_id_type=MESH)
 
-    pieces = x.shape[0] // STRIDE
-
-    def load_x(p):
-        rows = pl.ds(p * STRIDE, STRIDE)
-        return pltpu.make_async_copy(x_hbm.at[rows], x.at[rows], load_sem.at[p])
-
-    def load_pack():
-        return pltpu.make_async_copy(pack_hbm.at[me], pack, load_sem.at[pieces])
-
-    def load_table(c):
-        return pltpu.make_async_copy(table_hbm.at[me, c], table.at[c], table_sem.at[c])
-
-    for p in range(pieces):
-        load_x(p).start()
-    load_table(0).start()
-    load_pack().start()
-    for c in range(1, OWN):
-        load_table(c).start()
-    for p in range(pieces):
-        load_x(p).wait()
-        rows = pl.ds(p * STRIDE, STRIDE)
-        high, low = split(x[rows, :])
-        xh[rows, :] = high
-        xl[rows, :] = low
-    load_pack().wait()
 
     def halo_copy(c, side):
         return pltpu.make_async_remote_copy(
             src_ref=halo_out.at[c, side], dst_ref=halo_in.at[c, side],
-            send_sem=halo_ssem.at[c, side], recv_sem=halo_rsem.at[c, side],
+            send_sem=send_sem.at[0], recv_sem=halo_rsem.at[c],
             device_id=along(1 if side == 0 else -1), device_id_type=MESH,
         )
 
     def tile_copy(c, d):
         slot = (TM - d) % TM
-        rows = pl.ds(2, 6) if d == 4 else pl.ds(0, 8)
-        return pltpu.make_async_remote_copy(
-            src_ref=made.at[c, d, rows], dst_ref=got.at[c, slot, rows],
-            send_sem=send_sem.at[c, d], recv_sem=recv_sem.at[c, slot],
+        return pltpu.make_async_remote_copy(
+            src_ref=made.at[c, d], dst_ref=got.at[c, slot],
+            send_sem=send_sem.at[1], recv_sem=tile_rsem.at[c],
             device_id=along(d), device_id_type=MESH,
         )
 
+    def far_copy(c):
+        rows = pl.ds(2, 6)
+        return pltpu.make_async_remote_copy(
+            src_ref=made.at[c, 4, rows], dst_ref=got.at[c, 4, rows],
+            send_sem=send_sem.at[2], recv_sem=far_rsem.at[c],
+            device_id=along(4), device_id_type=MESH,
+        )
+
     def core_copy(c):
         return pltpu.make_async_remote_copy(
             src_ref=core_out.at[c], dst_ref=core_in.at[c],
-            send_sem=core_ssem.at[c], recv_sem=core_rsem.at[c],
+            send_sem=send_sem.at[3], recv_sem=core_rsem.at[c],
             device_id=mate, device_id_type=MESH,
         )
 
-    def chip_copy(c, n, i, j):
+    def chip_copy(c, i, j):
         return pltpu.make_async_remote_copy(
             src_ref=chip_all.at[c, chip], dst_ref=chip_all.at[c, chip],
-            send_sem=chip_ssem.at[c, n], recv_sem=chip_rsem.at[c, chip],
+            send_sem=send_sem.at[4], recv_sem=chip_rsem.at[c],
             device_id=across(i, j), device_id_type=MESH,
         )
 
-    def chip_arrival(c, n, i, j):
-        source = chip_of(i, j)
-        return pltpu.make_async_remote_copy(
-            src_ref=chip_all.at[c, source], dst_ref=chip_all.at[c, source],
-            send_sem=chip_ssem.at[c, n], recv_sem=chip_rsem.at[c, source],
-            device_id=across(i, j), device_id_type=MESH,
-        )
-
-    def make(c):
-        load_table(c).wait()
-        for n in range(points // 256):
+    def whole(ref, kind, sem):
+        return pltpu.make_async_remote_copy(
+            src_ref=ref, dst_ref=ref, send_sem=send_sem.at[kind], recv_sem=sem,
+            device_id=mate, device_id_type=MESH,
+        )
+
+    def make(c, opening=False):
+        if opening:
+            load_table().wait()
+        for n in range(pieces):
             columns = pl.ds(n * 256, 256)
+            if opening:
+                load_x(n).wait()
+                high, low = split(x[:, columns])
+                xh[:, columns] = high
+                xl[:, columns] = low
             both = dot(table[c], xh[:, columns])
             value = both[:80] + both[80:] + dot(table[c, :80, :], xl[:, columns])
             for d in range(TM):
@@ -229,11 +237,10 @@
     def send_first(c):
         halo_copy(c, 0).start()
         halo_copy(c, 1).start()
-        tile_copy(c, 4).start()
+        far_copy(c).start()
 
     def send_rest(c):
-        halo_copy(c, 0).wait_recv()
-        halo_copy(c, 1).wait_recv()
+        whole(halo_in.at[c], 0, halo_rsem.at[c]).wait_recv()
         first = me == 0
         last = me == TM - 1
         for d in range(4):
@@ -246,8 +253,8 @@
             tile_copy(c, d).start()
 
     def correlate(c):
-        for d in (4, 5, 3, 6, 2, 7, 1):
-            tile_copy(c, d).wait_recv()
+        far_copy(c).wait_recv()
+        whole(got.at[c, pl.ds(0, 6)], 1, tile_rsem.at[c]).wait_recv()
         own_rows = lax.broadcasted_iota(jnp.int32, (8, points), 0) < 2
         tiles = [made[c, 0]]
         for slot in range(1, TM):
@@ -265,43 +272,47 @@
         )
         even = gram[pl.ds(0, 32, stride=2), :]
         odd = gram[pl.ds(1, 32, stride=2), :]
-        core_out[c] = (
-            dot(even, pack[PACK_C0 : PACK_C0 + 64, :], precision=HIGHEST)
-            + dot(odd, pack[PACK_C1 : PACK_C1 + 64, :], precision=HIGHEST)
-        )
+        kept = even + dot(odd, pack[PACK_SWAP : PACK_SWAP + 64, :64], precision=HIGHEST)
+        core_out[c] = jnp.concatenate([kept[:16], kept[16:]], axis=1)
         core_copy(c).start()
 
     def spread(c):
         core_copy(c).wait_recv()
         chip_all[c, chip] = core_out[c] + core_in[c]
-        for n, (i, j) in enumerate(others):
-            chip_copy(c, n, i, j).start()
+        for i, j in others:
+            chip_copy(c, i, j).start()
 
     def finish(c):
-        for n, (i, j) in enumerate(others):
-            chip_arrival(c, n, i, j).wait_recv()
+        whole(chip_all.at[c, pl.ds(0, CHIPS - 1)], 4, chip_rsem.at[c]).wait_recv()
         parts = [chip_all[c, n] for n in range(CHIPS)]
         while len(parts) > 1:
             parts = [parts[n] + parts[n + 1] for n in range(0, len(parts), 2)]
         total = parts[0] / (points * 2 * CHIPS)
+        total = jnp.concatenate([total, pltpu.roll(total, 64, 1)], axis=0)
         rows = lax.broadcasted_iota(jnp.int32, total.shape, 0)
         lanes = lax.broadcasted_iota(jnp.int32, total.shape, 1)
         trace = jnp.sum(jnp.where(lanes == 2 * rows, total, 0.0)) + 1e-06
         scale = NB / trace
-        wide = jnp.concatenate([total, pltpu.roll(total, 64, 1)], axis=0)[:, :64]
+        odd = jnp.where(lanes % 2 == 0, -pltpu.roll(total, 127, 1), pltpu.roll(total, 1, 1))
+        wide = jnp.concatenate([total, odd], axis=0)[:, :64]
         one = scale * dot(pack[PACK_V0 : PACK_V0 + 8, :64], wide, NT, HIGHEST)
         two = scale * dot(one, wide, NN, HIGHEST)
         high, low = split(two)
         built = dot(high, ah[c]) + dot(high, al[c]) + dot(low, ah[c])
-        modes_ref[c] = built / NB
-        ordered = dot(total, pack[PACK_COL : PACK_COL + 128, :], precision=HIGHEST)
+        built = built / NB
+        modes_ref[c, 0] = built[:NMODE]
+        modes_ref[c, 1] = built[NMODE:]
+        ordered = dot(total[:, :64], pack[PACK_COL : PACK_COL + 64, :], precision=HIGHEST)
         ordered = dot(pack[PACK_ROW : PACK_ROW + 32, :32], ordered, precision=HIGHEST)
         cross_ref[c, 0] = ordered[:NB, :NB]
         cross_ref[c, 1] = pltpu.roll(ordered, 96, 1)[:NB, :NB]
 
-    make(0)
+    make(0, opening=True)
     pl.semaphore_wait(barrier, (TM - 1) + len(others) + 1)
     send_first(0)
+    load_pack().wait()
+    load_w().wait()
+    load_tables().wait()
 
     def step(s, carry):
         @pl.when(s < OWN)
@@ -318,25 +329,19 @@
             correlate(s - LAG)
             spread(s - LAG)
 
-        @pl.when(s >= LAG + 1)
+        @pl.when(s >= LAG + WAIT)
         def _():
-            finish(s - LAG - 1)
+            finish(s - LAG - WAIT)
 
         return carry
 
-    lax.fori_loop(1, OWN + LAG + 1, step, 0)
-
-    def drain(c, carry):
-        halo_copy(c, 0).wait_send()
-        halo_copy(c, 1).wait_send()
-        for d in range(1, TM):
-            tile_copy(c, d).wait_send()
-        core_copy(c).wait_send()
-        for n, (i, j) in enumerate(others):
-            chip_copy(c, n, i, j).wait_send()
-        return carry
-
-    lax.fori_loop(0, OWN, drain, 0)
+    lax.fori_loop(1, OWN + LAG + WAIT, step, 0)
+
+    whole(halo_out, 0, core_rsem.at[0]).wait_send()
+    whole(made.at[:, pl.ds(0, 6)], 1, core_rsem.at[0]).wait_send()
+    whole(made.at[:, 4, pl.ds(2, 6)], 2, core_rsem.at[0]).wait_send()
+    whole(core_out, 3, core_rsem.at[0]).wait_send()
+    whole(chip_all.at[:, pl.ds(0, CHIPS - 1)], 4, core_rsem.at[0]).wait_send()
 
 
 def local(snapshots, weights):
@@ -350,13 +355,14 @@
     modes, cross = pl.pallas_call(
         kernel,
         out_shape=(
-            jax.ShapeDtypeStruct((OWN, 2 * NMODE, points), F32),
+            jax.ShapeDtypeStruct((OWN, 2, NMODE, points), F32),
             jax.ShapeDtypeStruct((OWN, 2, NB, NB), F32),
         ),
-        in_specs=[any_space, vmem, any_space, any_space],
+        in_specs=[any_space, any_space, any_space, any_space],
         out_specs=(vmem, vmem),
         scratch_shapes=[
             pltpu.VMEM((steps, points), F32),
+            pltpu.VMEM((1, points), F32),
             pltpu.VMEM((steps, points), BF16),
             pltpu.VMEM((steps, points), BF16),
             pltpu.VMEM((OWN, rows, steps), BF16),
@@ -368,27 +374,25 @@
             pltpu.VMEM((OWN, 64, points), BF16),
             pltpu.VMEM((OWN, 64, points), BF16),
             pltpu.VMEM((64, 64), F32),
-            pltpu.VMEM((OWN, 32, 128), F32),
-            pltpu.VMEM((OWN, 32, 128), F32),
-            pltpu.VMEM((OWN, CHIPS, 32, 128), F32),
-            dma((steps // STRIDE + 1,)),
-            dma((OWN,)),
-            dma((OWN, 2)),
-            dma((OWN, 2)),
-            dma((OWN, TM)),
-            dma((OWN, TM)),
+            pltpu.VMEM((OWN, 16, 128), F32),
+            pltpu.VMEM((OWN, 16, 128), F32),
+            pltpu.VMEM((OWN, CHIPS, 16, 128), F32),
+            dma((points // 256 + 2,)),
+            dma((2,)),
+            dma((5,)),
             dma((OWN,)),
             dma((OWN,)),
-            dma((OWN, CHIPS)),
-            dma((OWN, CHIPS)),
+            dma((OWN,)),
+            dma((OWN,)),
+            dma((OWN,)),
         ],
         compiler_params=pltpu.CompilerParams(
-            collective_id=0, has_side_effects=True, vmem_limit_bytes=48 << 20
+            collective_id=0, has_side_effects=True, vmem_limit_bytes=52 << 20
         ),
         cost_estimate=pl.CostEstimate(flops=4 << 30, bytes_accessed=8 << 20, transcendentals=0),
         name="spod",
     )(snapshots, weights.reshape(1, points), table, pack)
-    return modes.reshape(OWN, 2, NMODE, points), cross
+    return modes, cross
 
 
 def solution(mesh):

time: 79 us -> 72.2 us (0.914)
  Pallas kernels: 73 us -> 68 us
  local copies, waits for them, and re-layouts: 5.22 us -> 3.38 us
    pallas_call x1, Pallas kernels: 73 us -> 68 us  [local(): pl.pallas_call(kernel, out_shape=(jax.ShapeDtypeStruct((OWN, 2, NMODE, po...]
    unnamed x7 -> x5, local copies, waits for them, and re-layouts: 4.45 us -> 2.48 us
    pallas_call x0 -> x1, local copies, waits for them, and re-layouts: none -> 0.89 us  [local(): pl.pallas_call(kernel, out_shape=(jax.ShapeDtypeStruct((OWN, 2, NMODE, po...]
where the time goes in v2:
time: 72.2 us; the launch traced here: 72 us
  Pallas kernels  68 us (94%)
  local copies, waits for them, and re-layouts  3.38 us (5%)
    pallas_call x1, Pallas kernels, local(): pl.pallas_call(kernel, out_shape=(jax.ShapeDtypeStruct((OWN, 2, NMODE, po...  68 us
    unnamed x5, local copies, waits for them, and re-layouts  2.48 us

profile of v2, /device:TPU:1, one launch (start us, length us, event | category | flops | bytes accessed | tf_op | source)
XLA Modules:
  0.0 72.0 jit_solution(6113057903171167944)
XLA Ops:
  0.6 0.0 copy-start
  0.6 0.7 copy-done
  1.3 0.0 copy-start.1
  1.3 1.1 %copy-done.1 = f32[8,168,128]{2,1,0:T(8,128)S(1)} copy-done((f32[8,168,128]{2,1,0:T(8,128)S(1)}, f32[8,168,128]{2,1,0:T(8,128)}, u32[]{:S(2)}) %copy-start.1) | copy-done | bytes 688152
  2.4 68.0 %spod.1 = (f32[8,2,4,1024]{3,2,1,0:T(4,128)S(1)}, f32[8,2,31,31]{3,2,1,0:T(8,128)S(1)}) custom-call(f32[512,1024]{1,0:T(8,128)} %x_hbm.1, f32[1,1024]{1,0:T(1,128)S(1)} %bitcast.1, bf16[8,8,160,512]{3,2,1,0:T(8,128)(2,1)} %constant.4.clone.table_hbm, f32[8,168,128]{2,1,0:T(8,128)S(1)} %copy-done.1), custom_call_target="tpu_custom_call" | custom-call | flops 4294967296 | bytes 8388608 | tf_op jit(solution)/shard_map/spod/pallas_call | solution.py:355
  70.4 0.9 %copy.6 = f32[8,2,31,31]{3,1,2,0:T(2,128)} copy(f32[8,2,31,31]{3,2,1,0:T(8,128)S(1)} %get-tuple-element.3) | data formatting | bytes 123008 | tf_op jit(solution)/shard_map/spod/pallas_call | solution.py:355
  71.3 0.7 copy.8
Async XLA Ops:
  0.6 0.7 copy-start
  1.3 1.1 %copy-start.1 = (f32[8,168,128]{2,1,0:T(8,128)S(1)}, f32[8,168,128]{2,1,0:T(8,128)}, u32[]{:S(2)}) copy-start(f32[8,168,128]{2,1,0:T(8,128)} %constant.5.clone.pack_hbm) | copy-start | bytes 2064388

commit v3 on v2

--- a/solution.py
+++ b/solution.py
@@ -20,6 +20,8 @@
 CHIPS = 16
 LAG = 2
 WAIT = 2
+ORDER = (0, 1, 2, 3, 7, 6, 5, 4)
+ORDERED = 7
 MESH = pl.DeviceIdType.MESH
 F32 = jnp.float32
 BF16 = jnp.bfloat16
@@ -82,10 +84,11 @@
 
 
 PACK_V0, PACK_COL, PACK_ROW, PACK_SWAP, PACK_END = 0, 8, 72, 104, 168
+PACK_WIDE = 1024
 
 
 def small_tables():
-    pack = np.zeros((TM, PACK_END, 128), np.float32)
+    pack = np.zeros((TM, PACK_END, PACK_WIDE), np.float32)
     b = np.arange(NB)
     m = np.arange(NMODE)
     basis = np.cos(np.pi * (b[:, None] + 0.5) * m[None, :] / NB)
@@ -148,7 +151,9 @@
         return pltpu.make_async_copy(x_hbm.at[:, columns], x.at[:, columns], load_sem.at[p])
 
     def load_pack():
-        return pltpu.make_async_copy(pack_hbm.at[me], pack, load_sem.at[pieces])
+        return pltpu.make_async_copy(
+            pack_hbm.at[me, :, pl.ds(0, 128)], pack, load_sem.at[pieces]
+        )
 
     def load_w():
         return pltpu.make_async_copy(w_hbm, w_ref, load_sem.at[pieces + 1])
@@ -182,7 +187,7 @@
         )
 
     def tile_copy(c, d):
-        slot = (TM - d) % TM
+        slot = lax.rem(TM - d, TM)
         return pltpu.make_async_remote_copy(
             src_ref=made.at[c, d], dst_ref=got.at[c, slot],
             send_sem=send_sem.at[1], recv_sem=tile_rsem.at[c],
@@ -237,7 +242,10 @@
     def send_first(c):
         halo_copy(c, 0).start()
         halo_copy(c, 1).start()
-        far_copy(c).start()
+
+        @pl.when(c < ORDERED)
+        def _():
+            far_copy(c).start()
 
     def send_rest(c):
         whole(halo_in.at[c], 0, halo_rsem.at[c]).wait_recv()
@@ -249,8 +257,23 @@
         for n, d in enumerate((4, 7, 6, 5)):
             total = made[c, d, 0:2, :] + halo_in[c, 1, 2 * n : 2 * n + 2, :]
             made[c, d, 0:2, :] = jnp.where(last, 0.0, total)
-        for d in (5, 3, 6, 2, 7, 1):
-            tile_copy(c, d).start()
+        @pl.when(c < ORDERED)
+        def _():
+            for d in (5, 3, 6, 2, 7, 1):
+                tile_copy(c, d).start()
+
+        @pl.when(c >= ORDERED)
+        def _():
+            for owner in ORDER:
+                d = lax.rem(owner - me + TM, TM)
+
+                @pl.when((d != 0) & (d != 4))
+                def _():
+                    tile_copy(c, d).start()
+
+                @pl.when(d == 4)
+                def _():
+                    far_copy(c).start()
 
     def correlate(c):
         far_copy(c).wait_recv()

time: 72.2 us -> 69.8 us (0.967)
  Pallas kernels: 68 us -> 66.8 us
  local copies, waits for them, and re-layouts: 3.38 us -> 2.28 us
    pallas_call x1, Pallas kernels: 68 us -> 66.8 us  [local(): pl.pallas_call(kernel, out_shape=(jax.ShapeDtypeStruct((OWN, 2, NMODE, po...]
    unnamed x5 -> x3, local copies, waits for them, and re-layouts: 2.48 us -> 1.38 us
where the time goes in v3:
time: 69.8 us; the launch traced here: 69.7 us
  Pallas kernels  66.8 us (96%)
  local copies, waits for them, and re-layouts  2.28 us (3%)
    pallas_call x1, Pallas kernels, local(): pl.pallas_call(kernel, out_shape=(jax.ShapeDtypeStruct((OWN, 2, NMODE, po...  66.8 us

profile of v3, /device:TPU:1, one launch (start us, length us, event | category | flops | bytes accessed | tf_op | source)
XLA Modules:
  0.0 69.7 jit_solution(1404446971342977268)
XLA Ops:
  0.6 0.0 copy-start
  0.6 0.7 copy-done
  1.3 66.8 %spod.1 = (f32[8,2,4,1024]{3,2,1,0:T(4,128)S(1)}, f32[8,2,31,31]{3,2,1,0:T(8,128)S(1)}) custom-call(f32[512,1024]{1,0:T(8,128)} %x_hbm.1, f32[1,1024]{1,0:T(1,128)S(1)} %bitcast.1, bf16[8,8,160,512]{3,2,1,0:T(8,128)(2,1)} %constant.4.clone.table_hbm, f32[8,168,1024]{2,1,0:T(8,128)} %constant.5.clone.pack_hbm), custom_call_target="tpu_custom_call" | custom-call | flops 4294967296 | bytes 8388608 | tf_op jit(solution)/shard_map/spod/pallas_call | solution.py:378
  68.1 0.9 %copy.6 = f32[8,2,31,31]{3,1,2,0:T(2,128)} copy(f32[8,2,31,31]{3,2,1,0:T(8,128)S(1)} %get-tuple-element.3) | data formatting | bytes 123008 | tf_op jit(solution)/shard_map/spod/pallas_call | solution.py:378
  69.0 0.7 %copy.8 = f32[8,2,4,1024]{3,2,1,0:T(4,128)} copy(f32[8,2,4,1024]{3,2,1,0:T(4,128)S(1)} %get-tuple-element.6) | data formatting | bytes 524288
Async XLA Ops:
  0.6 0.7 copy-start

commit v4 on v3

--- a/solution.py
+++ b/solution.py
@@ -22,6 +22,7 @@
 WAIT = 2
 ORDER = (0, 1, 2, 3, 7, 6, 5, 4)
 ORDERED = 7
+CHIP_ORDER = (0, 4, 1, 8, 12, 2, 3, 5, 13, 9, 7, 6, 15, 11, 14, 10)
 MESH = pl.DeviceIdType.MESH
 F32 = jnp.float32
 BF16 = jnp.bfloat16
@@ -83,8 +84,8 @@
     return [b % (NB + 1) for b in order]
 
 
-PACK_V0, PACK_COL, PACK_ROW, PACK_SWAP, PACK_END = 0, 8, 72, 104, 168
-PACK_WIDE = 1024
+PACK_V0, PACK_COL, PACK_ROW, PACK_END = 0, 8, 72, 104
+PACK_WIDE = 2048
 
 
 def small_tables():
@@ -92,10 +93,6 @@
     b = np.arange(NB)
     m = np.arange(NMODE)
     basis = np.cos(np.pi * (b[:, None] + 0.5) * m[None, :] / NB)
-    swap = np.zeros((64, 64), np.float32)
-    for i in range(32):
-        swap[2 * i + 1, 2 * i] = 1.0
-        swap[2 * i, 2 * i + 1] = -1.0
     for me in range(TM):
         for place, block in enumerate(block_order(me)):
             if block < NB:
@@ -104,13 +101,18 @@
             pack[me, PACK_COL + 2 * place, block] = 1.0
             pack[me, PACK_COL + 2 * place + 1, 32 + block] = 1.0
             pack[me, PACK_ROW + block, place] = 1.0
-        pack[me, PACK_SWAP : PACK_SWAP + 64, :64] = swap
     return pack
 
 
 def split(value):
     high = value.astype(BF16)
     return high, (value - high.astype(F32)).astype(BF16)
+
+
+def dot3(a, b, dims=NN):
+    ah, al = split(a)
+    bh, bl = split(b)
+    return dot(ah, bh, dims) + (dot(ah, bl, dims) + dot(al, bh, dims))
 
 
 def dot(a, b, dims=NN, precision=None):
@@ -209,11 +211,11 @@
             device_id=mate, device_id_type=MESH,
         )
 
-    def chip_copy(c, i, j):
+    def chip_copy(c, target):
         return pltpu.make_async_remote_copy(
             src_ref=chip_all.at[c, chip], dst_ref=chip_all.at[c, chip],
             send_sem=send_sem.at[4], recv_sem=chip_rsem.at[c],
-            device_id=across(i, j), device_id_type=MESH,
+            device_id=(me, target * 2 + core), device_id_type=MESH,
         )
 
     def whole(ref, kind, sem):
@@ -290,20 +292,24 @@
         ah[c] = high
         al[c] = low
         whigh, wlow = split(value * w_ref[...])
-        gram[...] = (
-            dot(high, whigh, NT) + dot(high, wlow, NT) + dot(low, whigh, NT)
-        )
+        product = dot(high, whigh, NT) + dot(high, wlow, NT) + dot(low, whigh, NT)
+        gram[...] = jnp.concatenate([product, product], axis=1)
         even = gram[pl.ds(0, 32, stride=2), :]
         odd = gram[pl.ds(1, 32, stride=2), :]
-        kept = even + dot(odd, pack[PACK_SWAP : PACK_SWAP + 64, :64], precision=HIGHEST)
+        lanes = lax.broadcasted_iota(jnp.int32, odd.shape, 1)
+        turned = jnp.where(lanes % 2 == 0, pltpu.roll(odd, 127, 1), -pltpu.roll(odd, 1, 1))
+        kept = (even + turned)[:, :64]
         core_out[c] = jnp.concatenate([kept[:16], kept[16:]], axis=1)
         core_copy(c).start()
 
     def spread(c):
         core_copy(c).wait_recv()
         chip_all[c, chip] = core_out[c] + core_in[c]
-        for i, j in others:
-            chip_copy(c, i, j).start()
+        for target in CHIP_ORDER:
+
+            @pl.when(target != chip)
+            def _():
+                chip_copy(c, target).start()
 
     def finish(c):
         whole(chip_all.at[c, pl.ds(0, CHIPS - 1)], 4, chip_rsem.at[c]).wait_recv()
@@ -318,8 +324,8 @@
         scale = NB / trace
         odd = jnp.where(lanes % 2 == 0, -pltpu.roll(total, 127, 1), pltpu.roll(total, 1, 1))
         wide = jnp.concatenate([total, odd], axis=0)[:, :64]
-        one = scale * dot(pack[PACK_V0 : PACK_V0 + 8, :64], wide, NT, HIGHEST)
-        two = scale * dot(one, wide, NN, HIGHEST)
+        one = scale * dot3(pack[PACK_V0 : PACK_V0 + 8, :64], wide, NT)
+        two = scale * dot3(one, wide)
         high, low = split(two)
         built = dot(high, ah[c]) + dot(high, al[c]) + dot(low, ah[c])
         built = built / NB
@@ -327,8 +333,8 @@
         modes_ref[c, 1] = built[NMODE:]
         ordered = dot(total[:, :64], pack[PACK_COL : PACK_COL + 64, :], precision=HIGHEST)
         ordered = dot(pack[PACK_ROW : PACK_ROW + 32, :32], ordered, precision=HIGHEST)
-        cross_ref[c, 0] = ordered[:NB, :NB]
-        cross_ref[c, 1] = pltpu.roll(ordered, 96, 1)[:NB, :NB]
+        cross_ref[c, :, 0, :] = ordered[:NB, :NB]
+        cross_ref[c, :, 1, :] = pltpu.roll(ordered, 96, 1)[:NB, :NB]
 
     make(0, opening=True)
     pl.semaphore_wait(barrier, (TM - 1) + len(others) + 1)
@@ -379,7 +385,7 @@
         kernel,
         out_shape=(
             jax.ShapeDtypeStruct((OWN, 2, NMODE, points), F32),
-            jax.ShapeDtypeStruct((OWN, 2, NB, NB), F32),
+            jax.ShapeDtypeStruct((OWN, NB, 2, NB), F32),
         ),
         in_specs=[any_space, any_space, any_space, any_space],
         out_specs=(vmem, vmem),
@@ -396,7 +402,7 @@
             pltpu.VMEM((OWN, TM, 8, points), F32),
             pltpu.VMEM((OWN, 64, points), BF16),
             pltpu.VMEM((OWN, 64, points), BF16),
-            pltpu.VMEM((64, 64), F32),
+            pltpu.VMEM((64, 128), F32),
             pltpu.VMEM((OWN, 16, 128), F32),
             pltpu.VMEM((OWN, 16, 128), F32),
             pltpu.VMEM((OWN, CHIPS, 16, 128), F32),
@@ -415,7 +421,7 @@
         cost_estimate=pl.CostEstimate(flops=4 << 30, bytes_accessed=8 << 20, transcendentals=0),
         name="spod",
     )(snapshots, weights.reshape(1, points), table, pack)
-    return modes, cross
+    return modes, cross.transpose(0, 2, 1, 3)
 
 
 def solution(mesh):

time: 69.8 us -> 69.2 us (level)
  Pallas kernels: 66.8 us -> 66 us
    pallas_call x1 -> x0, local copies, waits for them, and re-layouts: 0.89 us -> none  [local(): pl.pallas_call(kernel, out_shape=(jax.ShapeDtypeStruct((OWN, 2, NMODE, po...]
    pallas_call x1, Pallas kernels: 66.8 us -> 66 us  [local(): pl.pallas_call(kernel, out_shape=(jax.ShapeDtypeStruct((OWN, 2, NMODE, po...]
    unnamed x3 -> x4, local copies, waits for them, and re-layouts: 1.38 us -> 2.08 us
where the time goes in v4:
time: 69.2 us; the launch traced here: 68.7 us
  Pallas kernels  66 us (95%)
  local copies, waits for them, and re-layouts  2.08 us (3%)
    pallas_call x1, Pallas kernels, local(): pl.pallas_call(kernel, out_shape=(jax.ShapeDtypeStruct((OWN, 2, NMODE, po...  66 us
    unnamed x4, local copies, waits for them, and re-layouts  2.08 us

profile of v4, /device:TPU:1, one launch (start us, length us, event | category | flops | bytes accessed | tf_op | source)
XLA Modules:
  0.0 68.7 jit_solution(10572382618259570256)
XLA Ops:
  0.6 0.0 copy-start
  0.6 0.7 copy-done
  1.3 66.0 %spod.1 = (f32[8,2,4,1024]{3,2,1,0:T(4,128)S(1)}, f32[8,31,2,31]{3,2,1,0:T(2,128)S(1)}) custom-call(f32[512,1024]{1,0:T(8,128)} %x_hbm.1, f32[1,1024]{1,0:T(1,128)S(1)} %bitcast.3, bf16[8,8,160,512]{3,2,1,0:T(8,128)(2,1)} %constant.4.clone.table_hbm, f32[8,104,2048]{2,1,0:T(8,128)} %constant.5.clone.pack_hbm), custom_call_target="tpu_custom_call" | custom-call | flops 4294967296 | bytes 8388608 | tf_op jit(solution)/shard_map/spod/pallas_call | solution.py:384
  67.3 0.7 %copy.8 = f32[8,2,4,1024]{3,2,1,0:T(4,128)} copy(f32[8,2,4,1024]{3,2,1,0:T(4,128)S(1)} %get-tuple-element.8) | data formatting | bytes 524288
  68.0 0.7 %copy.9 = f32[8,2,31,31]{3,1,2,0:T(2,128)} copy(f32[8,2,31,31]{3,1,2,0:T(2,128)S(1)} %bitcast.2) | data formatting | bytes 123008
Async XLA Ops:
  0.6 0.7 %copy-start = (f32[1024]{0:T(1024)S(1)}, f32[1024]{0:T(1024)}, u32[]{:S(2)}) copy-start(f32[1024]{0:T(1024)} %param.5) | copy-start | bytes 12292

commit v5 on v4

--- a/solution.py
+++ b/solution.py
@@ -174,7 +174,7 @@
     load_w().start()
     load_tables().start()
     barrier = pltpu.get_barrier_semaphore()
-    for d in range(1, TM):
+    for d in (4, 3, 5, 2, 6, 1, 7):
         pl.semaphore_signal(barrier, inc=1, device_id=along(d), device_id_type=MESH)
     for i, j in others:
         pl.semaphore_signal(barrier, inc=1, device_id=across(i, j), device_id_type=MESH)
@@ -292,7 +292,8 @@
         ah[c] = high
         al[c] = low
         whigh, wlow = split(value * w_ref[...])
-        product = dot(high, whigh, NT) + dot(high, wlow, NT) + dot(low, whigh, NT)
+        both = dot(jnp.concatenate([high, low], axis=0), whigh, NT)
+        product = both[:64] + both[64:] + dot(high, wlow, NT)
         gram[...] = jnp.concatenate([product, product], axis=1)
         even = gram[pl.ds(0, 32, stride=2), :]
         odd = gram[pl.ds(1, 32, stride=2), :]

time: 69.2 us -> 69.2 us (level)
  no operation moved by 1% of the time
where the time goes in v5:
time: 69.2 us; the launch traced here: 68.7 us
  Pallas kernels  66 us (95%)
  local copies, waits for them, and re-layouts  2.08 us (3%)
    pallas_call x1, Pallas kernels, local(): pl.pallas_call(kernel, out_shape=(jax.ShapeDtypeStruct((OWN, 2, NMODE, po...  66 us
    unnamed x4, local copies, waits for them, and re-layouts  2.08 us

profile of v5, /device:TPU:1, one launch (start us, length us, event | category | flops | bytes accessed | tf_op | source)
XLA Modules:
  0.0 68.7 jit_solution(12368241351801565573)
XLA Ops:
  0.6 0.0 copy-start
  0.6 0.7 copy-done
  1.3 66.0 %spod.1 = (f32[8,2,4,1024]{3,2,1,0:T(4,128)S(1)}, f32[8,31,2,31]{3,2,1,0:T(2,128)S(1)}) custom-call(f32[512,1024]{1,0:T(8,128)} %x_hbm.1, f32[1,1024]{1,0:T(1,128)S(1)} %bitcast.3, bf16[8,8,160,512]{3,2,1,0:T(8,128)(2,1)} %constant.4.clone.table_hbm, f32[8,104,2048]{2,1,0:T(8,128)} %constant.5.clone.pack_hbm), custom_call_target="tpu_custom_call" | custom-call | flops 4294967296 | bytes 8388608 | tf_op jit(solution)/shard_map/spod/pallas_call | solution.py:385
  67.3 0.7 %copy.8 = f32[8,2,4,1024]{3,2,1,0:T(4,128)} copy(f32[8,2,4,1024]{3,2,1,0:T(4,128)S(1)} %get-tuple-element.8) | data formatting | bytes 524288
  68.0 0.7 %copy.9 = f32[8,2,31,31]{3,1,2,0:T(2,128)} copy(f32[8,2,31,31]{3,1,2,0:T(2,128)S(1)} %bitcast.2) | data formatting | bytes 123008
Async XLA Ops:
  0.6 0.7 %copy-start = (f32[1024]{0:T(1024)S(1)}, f32[1024]{0:T(1024)}, u32[]{:S(2)}) copy-start(f32[1024]{0:T(1024)} %param.5) | copy-start | bytes 12292
